TPU v7x, 256 devices: a whole 4x4x8 slice. The times are simulated.
256 devices in a mesh: dev: 256 (over y, z, x, core).
Axes of the slice: x: 4, y: 4, z: 8, core: 2. Of those that a mesh axis runs over, the one named last changes fastest.
Arguments:
- block_in: float32 [2048, 4096], P('dev'), may hold values from -6 to 6
- leaf_basis: float32 [2048, 2048], P('dev'), may hold values from -0.75 to 0.75
- transfer: float32 [3840, 1024], P('dev'), may hold values from -0.875 to 0.875
- upper_transfer: float32 [252, 1024], replicated, may hold values from -0.875 to 0.875
- near_count: int32 [2048], P('dev'), may hold values from 1 to 12, as said below
- near_partner: int32 [2048, 12], P('dev'), may hold values from 0 to 2047, as said below
- near_block: float32 [2048, 12, 4096], P('dev'), may hold values from -0.3125 to 0.3125
- far_count: int32 [3840], P('dev'), may hold values from 1 to 8, as said below
- far_partner: int32 [3840, 8], P('dev'), may hold values from 0 to 2047, as said below
- coupling: float32 [3840, 8, 1024], P('dev'), may hold values from -0.21875 to 0.21875
- upper_pair: int32 [1024, 2], P('dev'), may hold values from 0 to 253, as said below
- upper_block: float32 [1024, 1024], P('dev'), may hold values from -0.21875 to 0.21875
Outputs:
- first_image: float32 [2048, 4096], P('dev')
- second_image: float32 [2048, 4096], P('dev')
Inputs may be any that keep to these rules, and one draw needn't show every extreme that they name: `near_partner`: slot 0 of leaf t's list is t itself; every listed leaf lies within 2 leaves of t. Only the first near_count[t] slots of a leaf's list and blocks count; some leaf uses all of them. `far_partner`: row r of local cluster (j, p) names clusters p2 of level j, p2 != p, with |p2 - p| at most the number of level-j clusters that one device holds. Only the first far_count[r] slots of a cluster's list and couplings count; some cluster uses all of them. `upper_pair`: column 0 is the target and column 1 the source of a block, both in the upper numbering; they lie in the same level and differ.
All inputs are finite; a program needn't handle non-finite values.
Results may differ from a plain program's by a relative error of at most 0.0003.
Values sent between devices are 32-bit elements; how exact they have to be, the bound alone decides.
No kernel may reach another device: no remote copies, remote signals or barrier semaphores. Data moves between devices by JAX's collectives and lax.ppermute only.
A program may use at most 192 MiB of HBM per device.

v0:
```python
import jax
import jax.numpy as jnp
import numpy as np
from jax import lax
from jax.sharding import PartitionSpec as P

NRHS = 64
LEAF = 64
RANK = 32
NEARP = 12
FARP = 8
L_DEV = 8
CPD = 15
NW = 2


highest = lax.Precision.HIGHEST


def extended(array, sides, width):
    for axis, dim in sides:
        peers, length = (lax.axis_size(axis), array.shape[dim])
        up = [(i, (i + 1) % peers) for i in range(peers - 1)]
        down = [(j, i) for i, j in up]
        last = lax.slice_in_dim(array, length - width, length, axis=dim)
        leading = lax.slice_in_dim(array, 0, width, axis=dim)
        before = lax.ppermute(last, axis, up)
        after = lax.ppermute(leading, axis, down)
        array = jnp.concatenate([before, array, after], axis=dim)
    return array


def product(form, left, right):
    return jnp.einsum(form, left, right, precision=highest)


def level_rows(height):
    breadth = L_DEV >> height
    return (breadth, 2 * L_DEV - 2 * breadth)


def level_tables():
    breadth_list = []
    offset_list = []
    for height in range(L_DEV.bit_length()):
        breadth, offset = level_rows(height)
        breadth_list = breadth_list + [breadth] * breadth
        offset_list = offset_list + [offset] * breadth
    return (
        jnp.asarray(np.array(breadth_list, np.int32)),
        jnp.asarray(np.array(offset_list, np.int32)),
    )


def lift_pairs(weights, coefficients):
    lifted = product("qab,qar->qbr", weights, coefficients)
    return lifted[0::2] + lifted[1::2]


def push_down(weights, coarse, local_terms):
    return local_terms + product("qab,qbr->qar", weights, jnp.repeat(coarse, 2, axis=0))


def descend_branch(summed, upper_transfer, level_sizes, devices, my_index):
    parent_down = lax.dynamic_index_in_dim(
        summed, devices - 4 + my_index // (devices // 2), 0, keepdims=False
    )
    for clusters in reversed(level_sizes[:-1]):
        ancestor = devices - 2 * clusters + my_index // (devices // clusters)
        ancestor_link = lax.dynamic_index_in_dim(
            upper_transfer, ancestor, 0, keepdims=False
        ).reshape(RANK, RANK)
        parent_down = lax.dynamic_index_in_dim(summed, ancestor, 0, keepdims=False) + product(
            "ab,br->ar", ancestor_link, parent_down
        )
    return parent_down


def apply_operator(vectors, operands):
    (
        leaf_basis,
        transfer,
        upper_transfer,
        near_count,
        near_partner,
        near_block,
        far_count,
        far_partner,
        coupling,
        upper_pair,
        upper_block,
    ) = operands
    devices = lax.axis_size("dev")
    my_index = lax.axis_index("dev")
    levels = L_DEV.bit_length()
    near_rim = extended(vectors, (("dev", 0),), NW)
    leaf_rows = vectors.reshape(L_DEV, LEAF, NRHS)
    leaf_bases = leaf_basis.reshape(L_DEV, LEAF, RANK)
    transfers = transfer.reshape(CPD, RANK, RANK)
    coefficients = [product("tik,tir->tkr", leaf_bases, leaf_rows)]
    for height in range(1, levels):
        breadth, offset = level_rows(height - 1)
        coefficients.append(lift_pairs(transfers[offset : offset + breadth], coefficients[-1]))
    joined = jnp.concatenate(
        [level_block.reshape(level_block.shape[0], RANK * NRHS) for level_block in coefficients],
        axis=0,
    )
    far_rim = extended(joined, (("dev", 0),), CPD)
    top_link = transfers[CPD - 1]
    parent_share = product("ab,ar->br", top_link, coefficients[-1][0])
    gathered = lax.all_gather(
        parent_share.reshape(1, RANK * NRHS), "dev", axis=0, tiled=True
    ).reshape(devices, RANK, NRHS)
    level_sizes = [devices >> halving for halving in range(1, devices.bit_length() - 1)]
    upper_levels = [gathered[0::2] + gathered[1::2]]
    for clusters in level_sizes[:-1]:
        offset = devices - 2 * clusters
        weights = upper_transfer[offset : offset + clusters].reshape(clusters, RANK, RANK)
        upper_levels.append(lift_pairs(weights, upper_levels[-1]))
    upper_all = jnp.concatenate(upper_levels, axis=0)
    coupled = product(
        "nab,nbr->nar",
        upper_block.reshape(-1, RANK, RANK),
        jnp.take(upper_all, upper_pair[:, 1], axis=0),
    )
    one_hot = (upper_pair[:, 0][:, None] == jnp.arange(upper_all.shape[0])[None, :]).astype(
        jnp.float32
    )
    upper_far = product("nu,nar->uar", one_hot, coupled)
    summed = lax.psum(upper_far.reshape(-1, RANK * NRHS), "dev").reshape(-1, RANK, NRHS)
    parent_down = descend_branch(summed, upper_transfer, level_sizes, devices, my_index)
    breadths, offsets = level_tables()
    owner_index = far_partner // breadths[:, None]
    position = (
        (owner_index - my_index + 1) * CPD + offsets[:, None] + far_partner % breadths[:, None]
    )
    picked = jnp.take(far_rim, position, axis=0).reshape(CPD, FARP, RANK, NRHS)
    live_mask = (jnp.arange(FARP)[None, :] < far_count[:, None]).astype(jnp.float32)
    far_terms = product(
        "psab,psbr->par",
        coupling.reshape(CPD, FARP, RANK, RANK) * live_mask[:, :, None, None],
        picked,
    )
    downward = far_terms[CPD - 1 : CPD] + product("ab,br->ar", top_link, parent_down)[None]
    for height in range(levels - 1, 0, -1):
        breadth, offset = level_rows(height - 1)
        downward = push_down(
            transfers[offset : offset + breadth], downward, far_terms[offset : offset + breadth]
        )
    local_index = near_partner - (my_index * L_DEV - NW)
    picked_rows = jnp.take(near_rim, local_index, axis=0).reshape(L_DEV, NEARP, LEAF, NRHS)
    near_mask = (jnp.arange(NEARP)[None, :] < near_count[:, None]).astype(jnp.float32)
    near_terms = product(
        "tsij,tsjr->tir",
        near_block.reshape(L_DEV, NEARP, LEAF, LEAF) * near_mask[:, :, None, None],
        picked_rows,
    )
    image_rows = product("tik,tkr->tir", leaf_bases, downward) + near_terms
    return image_rows.reshape(L_DEV, LEAF * NRHS)


def body(
    block_in,
    leaf_basis,
    transfer,
    upper_transfer,
    near_count,
    near_partner,
    near_block,
    far_count,
    far_partner,
    coupling,
    upper_pair,
    upper_block,
):
    operands = (
        leaf_basis,
        transfer,
        upper_transfer,
        near_count,
        near_partner,
        near_block,
        far_count,
        far_partner,
        coupling,
        upper_pair,
        upper_block,
    )
    first_image = apply_operator(block_in, operands)
    second_image = apply_operator(first_image, operands)
    return (first_image, second_image)


def solution(mesh):
    in_specs = (
        P("dev", None),
        P("dev", None),
        P("dev", None),
        P(),
        P("dev"),
        P("dev", None),
        P("dev", None, None),
        P("dev"),
        P("dev", None),
        P("dev", None, None),
        P("dev", None),
        P("dev", None),
    )
    out_specs = (P("dev", None), P("dev", None))
    return jax.shard_map(body, mesh=mesh, in_specs=in_specs, out_specs=out_specs, check_vma=False)
```

profile of v0, /device:TPU:2, one launch (start us, length us, event | category | flops | bytes accessed | tf_op | source)
XLA Modules:
  0.0 996.9 jit_solution(15834956306020463969)
XLA Ops:
  15.8 1.9 collective-permute-start
  17.7 3.6 collective-permute-start.1
  22.1 2.6 collective-permute-start.3
  24.6 2.1 collective-permute-start.2
  32.9 2.4 reshape.261
  36.0 2.9 reshape.233
  39.6 2.1 copy.215
  41.6 4.0 copy.148
  46.7 2.8 copy.150
  57.1 2.4 gather_fusion.2
  59.5 2.7 reshape.355
  62.2 3.2 broadcast_select_fusion.1
  65.4 3.6 reshape.371
  69.0 52.6 %all-gather.5.cloned.1.call-done = f32[256,1,2048]{2,1,0:T(1,128)} async-done(((f32[1,1,2048]{2,1,0:T(1,128)}), f32[256,1,2048]{2,1,0:T(1,128)}) %all-gather.5.cloned.1.call-update) | async-done | bytes 2097168 | tf_op jit(solution)/shard_map/all_gather | solution.py:111
  121.6 6.0 copy.144
  127.6 36.4 %slice.248 = f32[128,32,64]{0,2,1:T(8,128)} slice(f32[256,32,64]{0,2,1:T(8,128)} %bitcast.214), slice={[0:256:2], [0:32:1], [0:64:1]} | slice | bytes 2097152 | tf_op jit(solution)/shard_map/slice | solution.py:115
  164.1 36.8 %slice.249 = f32[128,32,64]{0,2,1:T(8,128)} slice(f32[256,32,64]{0,2,1:T(8,128)} %bitcast.215), slice={[1:256:2], [0:32:1], [0:64:1]} | slice | bytes 2097152 | tf_op jit(solution)/shard_map/slice | solution.py:115
  200.9 4.0 copy.213
  204.9 4.1 copy.214
  209.0 4.2 add_dynamic-update-slice_fusion.1
  213.7 2.2 convolution_bitcast_fusion.1
  224.5 2.8 gather_fusion.1
  227.6 2.4 fusion.40
  230.3 7.9 fusion.10
  238.2 4.5 concatenate.27
  242.7 2.1 gather_fusion
  244.8 2.3 bitcast_select_fusion.1
  247.1 3.0 reshape.240
  250.1 6.2 fusion.12
  256.3 234.4 %all-reduce.3.cloned.1.call-done = f32[254,32,64]{0,2,1:T(8,128)} async-done(((f32[254,32,64]{0,2,1:T(8,128)}), f32[254,32,64]{0,2,1:T(8,128)}) %all-reduce.3.cloned.1.call-update) | async-done | bytes 2080784 | tf_op jit(solution)/shard_map/psum | solution.py:130
  490.8 7.9 dynamic-slice_reduce_fusion.7
  508.3 1.5 reshape.265
  509.8 1.5 fusion.75
  511.3 1.6 copy.181
  512.9 1.5 slice.298
  514.4 1.9 collective-permute-start.7
  516.3 1.6 copy.180
  517.9 1.5 slice.296
  519.4 2.4 collective-permute-start.6
  521.9 1.6 reshape.264
  523.5 1.6 pad_maximum_fusion.3
  525.9 3.0 collective-permute-start.4
  528.9 2.6 collective-permute-start.5
  531.4 1.7 reshape.263
  534.1 2.4 gather_fusion.5
  536.5 3.1 reshape.365
  539.6 3.1 broadcast_select_fusion
  542.8 3.6 reshape.372
  546.4 62.3 %all-gather.7.cloned.1.call-done = f32[256,1,2048]{2,1,0:T(1,128)} async-done(((f32[1,1,2048]{2,1,0:T(1,128)}), f32[256,1,2048]{2,1,0:T(1,128)}) %all-gather.7.cloned.1.call-update) | async-done | bytes 2097168 | tf_op jit(solution)/shard_map/all_gather | solution.py:111
  608.6 6.0 copy.169
  614.7 36.4 %slice.281 = f32[128,32,64]{0,2,1:T(8,128)} slice(f32[256,32,64]{0,2,1:T(8,128)} %bitcast.216), slice={[0:256:2], [0:32:1], [0:64:1]} | slice | bytes 2097152 | tf_op jit(solution)/shard_map/slice | solution.py:115
  651.1 36.6 %slice.282 = f32[128,32,64]{0,2,1:T(8,128)} slice(f32[256,32,64]{0,2,1:T(8,128)} %bitcast.217), slice={[1:256:2], [0:32:1], [0:64:1]} | slice | bytes 2097152 | tf_op jit(solution)/shard_map/slice | solution.py:115
  687.7 4.0 copy.217
  691.7 4.1 copy.218
  695.8 4.2 add_dynamic-update-slice_fusion
  700.5 2.2 convolution_bitcast_fusion
  710.9 2.8 gather_fusion.4
  714.9 3.1 fusion.38
  718.0 7.4 fusion.11
  725.4 4.5 concatenate.31
  732.2 3.0 reshape.268
  735.2 4.9 fusion.15
  740.2 238.5 %all-reduce.5.cloned.1.call-done = f32[254,32,64]{0,2,1:T(8,128)} async-done(((f32[254,32,64]{0,2,1:T(8,128)}), f32[254,32,64]{0,2,1:T(8,128)}) %all-reduce.5.cloned.1.call-update) | async-done | bytes 2080784 | tf_op jit(solution)/shard_map/psum | solution.py:130
  978.7 8.1 dynamic-slice_reduce_fusion
  (312 shorter events, 60.8 us)
Async XLA Ops:
  7.2 20.3 %copy-start.80 = (s32[15]{0:T(128)S(1)}, s32[15]{0:T(128)}, u32[]{:S(2)}) copy-start(s32[15]{0:T(128)} %constant.236.clone) | copy-start | bytes 184
  7.2 20.2 %copy-start.81 = (s32[15]{0:T(128)S(1)}, s32[15]{0:T(128)}, u32[]{:S(2)}) copy-start(s32[15]{0:T(128)} %constant.260) | copy-start | bytes 184
  7.2 14.2 %copy-start.29 = (f32[8,4096]{1,0:T(8,128)S(1)}, f32[8,4096]{1,0:T(8,128)}, u32[]{:S(2)}) copy-start(f32[8,4096]{1,0:T(8,128)} %param.26) | copy-start | bytes 393220
  7.2 19.5 %copy-start.74 = (s32[8,12]{1,0:T(8,128)S(1)}, s32[8,12]{1,0:T(8,128)}, u32[]{:S(2)}) copy-start(s32[8,12]{1,0:T(8,128)} %param.31) | copy-start | bytes 1156
  7.2 20.2 %copy-start.75 = (s32[15,8]{0,1:T(8,128)S(1)}, s32[15,8]{0,1:T(8,128)}, u32[]{:S(2)}) copy-start(s32[15,8]{0,1:T(8,128)} %param.34) | copy-start | bytes 1444
  7.3 21.7 %copy-start.82 = (s32[4,2]{0,1:T(2,128)S(1)}, s32[4,2]{0,1:T(2,128)}, u32[]{:S(2)}) copy-start(s32[4,2]{0,1:T(2,128)} %param.36) | copy-start | bytes 100
  7.3 22.8 %copy-start.78 = (s32[8]{0:T(128)S(1)}, s32[8]{0:T(128)}, u32[]{:S(2)}) copy-start(s32[8]{0:T(128)} %param.30) | copy-start | bytes 100
  7.3 23.4 %copy-start.79 = (s32[15]{0:T(128)S(1)}, s32[15]{0:T(128)}, u32[]{:S(2)}) copy-start(s32[15]{0:T(128)} %param.33) | copy-start | bytes 184
  7.3 114.3 %all-gather.5.cloned.1.call-start = ((), (), s32[]{:S(2)}) async-start(), calls=%async_computation.2 | async-start | bytes 2105344 | tf_op jit(solution)/shard_map/all_gather | solution.py:111
  9.1 23.8 %copy-start.30 = (f32[2,32,32]{2,1,0:T(8,128)}, f32[2,32,32]{2,1,0:T(8,128)S(1)}, u32[]{:S(2)}) copy-start(f32[2,32,32]{2,1,0:T(8,128)S(1)} %slice.239) | copy-start | bytes 24580
  10.0 22.8 %copy-start.9 = (f32[8,64,32]{2,1,0:T(8,128)}, f32[8,64,32]{2,1,0:T(8,128)S(1)}, u32[]{:S(2)}) copy-start(f32[8,64,32]{2,1,0:T(8,128)S(1)} %reshape.234) | copy-start | bytes 196612
  11.2 21.6 %copy-start.14 = (f32[8,32,32]{2,1,0:T(8,128)}, f32[8,32,32]{2,1,0:T(8,128)S(1)}, u32[]{:S(2)}) copy-start(f32[8,32,32]{2,1,0:T(8,128)S(1)} %slice.231) | copy-start | bytes 98308
  12.3 20.5 %copy-start.20 = (f32[4,32,32]{2,1,0:T(8,128)}, f32[4,32,32]{2,1,0:T(8,128)S(1)}, u32[]{:S(2)}) copy-start(f32[4,32,32]{2,1,0:T(8,128)S(1)} %slice.235) | copy-start | bytes 49156
  14.7 476.1 %all-reduce.3.cloned.1.call-start = ((), (), s32[]{:S(2)}) async-start(), calls=%async_computation | async-start | bytes 4194304 | tf_op jit(solution)/shard_map/psum | solution.py:130
  14.8 18.0 %copy-start.59 = (f32[1,2048]{1,0:T(1,128)}, f32[1,2048]{1,0:T(1,128)S(1)}, u32[]{:S(2)}) copy-start(f32[1,2048]{1,0:T(1,128)S(1)} %reshape.239) | copy-start | bytes 24580
  14.9 17.9 %copy-start.40 = (f32[2,2048]{1,0:T(2,128)}, f32[2,2048]{1,0:T(2,128)S(1)}, u32[]{:S(2)}) copy-start(f32[2,2048]{1,0:T(2,128)S(1)} %reshape.238) | copy-start | bytes 49156
  15.0 17.8 %copy-start.39 = (f32[4,2048]{1,0:T(4,128)}, f32[4,2048]{1,0:T(4,128)S(1)}, u32[]{:S(2)}) copy-start(f32[4,2048]{1,0:T(4,128)S(1)} %reshape.237) | copy-start | bytes 98308
  15.1 17.7 %copy-start.37 = (f32[8,2048]{1,0:T(8,128)}, f32[8,2048]{1,0:T(8,128)S(1)}, u32[]{:S(2)}) copy-start(f32[8,2048]{1,0:T(8,128)S(1)} %reshape.236) | copy-start | bytes 196612
  15.8 222.4 %collective-permute-start = (f32[15,2048]{1,0:T(8,128)}, f32[15,2048]{1,0:T(8,128)}, u32[]{:S(2)}, u32[]{:S(2)}) collective-permute-start(f32[15,2048]{1,0:T(8,128)} %pad_maximum_fusion.2), channel_id=1, source_target_pairs={{0,1},{1,2},{2,3},{3,4},{4,5},{5,6},{6,7},{7,8},{8,9},{9,10},{10,1... | collective-permute-start | bytes 368648 | tf_op jit(solution)/shard_map/ppermute | solution.py:27
  17.7 220.4 %collective-permute-start.1 = (f32[15,2048]{1,0:T(8,128)}, f32[15,2048]{1,0:T(8,128)}, u32[]{:S(2)}, u32[]{:S(2)}) collective-permute-start(f32[15,2048]{1,0:T(8,128)} %pad_maximum_fusion.2), channel_id=1, source_target_pairs={{1,0},{2,1},{3,2},{4,3},{5,4},{6,5},{7,6},{8,7},{9,8},{10,9},{11,1... | collective-permute-start | bytes 368648 | tf_op jit(solution)/shard_map/ppermute | solution.py:28
  22.1 34.1 %collective-permute-start.3 = (f32[2,4096]{1,0:T(2,128)}, f32[2,4096]{1,0:T(2,128)}, u32[]{:S(2)}, u32[]{:S(2)}) collective-permute-start(f32[2,4096]{1,0:T(2,128)} %get-tuple-element.36), channel_id=1, source_target_pairs={{1,0},{2,1},{3,2},{4,3},{5,4},{6,5},{7,6},{8,7},{9,8},{10,9},{11,1... | collective-permute-start | bytes 98312 | tf_op jit(solution)/shard_map/ppermute | solution.py:28
  24.6 31.6 %collective-permute-start.2 = (f32[2,4096]{1,0:T(2,128)}, f32[2,4096]{1,0:T(2,128)}, u32[]{:S(2)}, u32[]{:S(2)}) collective-permute-start(f32[2,4096]{1,0:T(2,128)} %get-tuple-element.35), channel_id=1, source_target_pairs={{0,1},{1,2},{2,3},{3,4},{4,5},{5,6},{6,7},{7,8},{8,9},{9,10},{10,1... | collective-permute-start | bytes 98312 | tf_op jit(solution)/shard_map/ppermute | solution.py:27
  38.8 6.8 slice-start
  41.6 7.9 slice-start.1
  46.6 6.2 copy-start.70
  46.6 6.8 copy-start.69
  46.7 7.5 copy-start.68
  46.7 8.2 copy-start.67
  46.7 8.8 copy-start.66
  51.4 171.1 %copy-start.23 = (f32[8,32,32]{2,1,0:T(8,128)}, f32[8,32,32]{2,1,0:T(8,128)S(1)}, u32[]{:S(2)}) copy-start(f32[8,32,32]{2,1,0:T(8,128)S(1)} %reshape.247) | copy-start | bytes 98308
  219.4 7.9 copy-start.33
  219.4 7.9 copy-start.77
  219.5 8.2 copy-start.76
  230.0 8.1 copy-start.41
  230.1 378.6 %all-gather.7.cloned.1.call-start = ((), (), s32[]{:S(2)}) async-start(), calls=%async_computation.3 | async-start | bytes 2105344 | tf_op jit(solution)/shard_map/all_gather | solution.py:111
  256.3 243.3 %copy-start.43 = (f32[32,32]{1,0:T(8,128)S(1)}, f32[32,32]{1,0:T(8,128)}, u32[]{:S(2)}) copy-start(f32[32,32]{1,0:T(8,128)} %copy-done.42) | copy-start | bytes 12292
  256.3 243.9 %copy-start.15 = (f32[8,32,32]{2,1,0:T(8,128)S(1)}, f32[8,32,32]{2,1,0:T(8,128)}, u32[]{:S(2)}) copy-start(f32[8,32,32]{2,1,0:T(8,128)} %copy-done.14) | copy-start | bytes 98308
  256.3 244.1 %copy-start.10 = (f32[8,64,32]{2,1,0:T(8,128)S(1)}, f32[8,64,32]{2,1,0:T(8,128)}, u32[]{:S(2)}) copy-start(f32[8,64,32]{2,1,0:T(8,128)} %copy-done.9) | copy-start | bytes 196612
  490.7 7.9 copy-start.55
  490.7 8.1 copy-start.53
  490.8 8.2 copy-start.51
  490.8 8.4 copy-start.49
  490.8 8.6 copy-start.47
  490.8 8.7 copy-start.45
  490.8 8.9 copy-start.28
  490.8 9.0 copy-start.31
  490.8 9.2 copy-start.21
  490.8 9.7 copy-start.27
  502.2 22.8 %copy-start.17 = (f32[8,64,64]{1,2,0:T(8,128)S(1)}, f32[8,64,64]{1,2,0:T(8,128)}, u32[]{:S(2)}) copy-start(f32[8,64,64]{1,2,0:T(8,128)} %copy-done.16) | copy-start | bytes 393220
  506.0 472.7 %all-reduce.5.cloned.1.call-start = ((), (), s32[]{:S(2)}) async-start(), calls=%async_computation.1 | async-start | bytes 4194304 | tf_op jit(solution)/shard_map/psum | solution.py:130
  514.4 18.7 %collective-permute-start.7 = (f32[2,4096]{1,0:T(2,128)}, f32[2,4096]{1,0:T(2,128)}, u32[]{:S(2)}, u32[]{:S(2)}) collective-permute-start(f32[2,4096]{1,0:T(2,128)} %slice.298), channel_id=1, source_target_pairs={{1,0},{2,1},{3,2},{4,3},{5,4},{6,5},{7,6},{8,7},{9,8},{10,9},{11,1... | collective-permute-start | bytes 98312 | tf_op jit(solution)/shard_map/ppermute | solution.py:28
  519.4 13.7 %collective-permute-start.6 = (f32[2,4096]{1,0:T(2,128)}, f32[2,4096]{1,0:T(2,128)}, u32[]{:S(2)}, u32[]{:S(2)}) collective-permute-start(f32[2,4096]{1,0:T(2,128)} %slice.296), channel_id=1, source_target_pairs={{0,1},{1,2},{2,3},{3,4},{4,5},{5,6},{6,7},{7,8},{8,9},{9,10},{10,1... | collective-permute-start | bytes 98312 | tf_op jit(solution)/shard_map/ppermute | solution.py:27
  525.9 199.5 %collective-permute-start.4 = (f32[15,2048]{1,0:T(8,128)}, f32[15,2048]{1,0:T(8,128)}, u32[]{:S(2)}, u32[]{:S(2)}) collective-permute-start(f32[15,2048]{1,0:T(8,128)} %pad_maximum_fusion.3), channel_id=1, source_target_pairs={{0,1},{1,2},{2,3},{3,4},{4,5},{5,6},{6,7},{7,8},{8,9},{9,10},{10,1... | collective-permute-start | bytes 368648 | tf_op jit(solution)/shard_map/ppermute | solution.py:27
  528.9 196.5 %collective-permute-start.5 = (f32[15,2048]{1,0:T(8,128)}, f32[15,2048]{1,0:T(8,128)}, u32[]{:S(2)}, u32[]{:S(2)}) collective-permute-start(f32[15,2048]{1,0:T(8,128)} %pad_maximum_fusion.3), channel_id=1, source_target_pairs={{1,0},{2,1},{3,2},{4,3},{5,4},{6,5},{7,6},{8,7},{9,8},{10,9},{11,1... | collective-permute-start | bytes 368648 | tf_op jit(solution)/shard_map/ppermute | solution.py:28
  740.1 246.8 %copy-start.56 = (f32[32,32]{1,0:T(8,128)S(1)}, f32[32,32]{1,0:T(8,128)}, u32[]{:S(2)}) copy-start(f32[32,32]{1,0:T(8,128)} %reshape.257) | copy-start | bytes 12292
  740.1 246.9 %copy-start.54 = (f32[32,32]{1,0:T(8,128)S(1)}, f32[32,32]{1,0:T(8,128)}, u32[]{:S(2)}) copy-start(f32[32,32]{1,0:T(8,128)} %reshape.256) | copy-start | bytes 12292
  740.1 247.0 %copy-start.52 = (f32[32,32]{1,0:T(8,128)S(1)}, f32[32,32]{1,0:T(8,128)}, u32[]{:S(2)}) copy-start(f32[32,32]{1,0:T(8,128)} %reshape.255) | copy-start | bytes 12292
  740.1 247.2 %copy-start.50 = (f32[32,32]{1,0:T(8,128)S(1)}, f32[32,32]{1,0:T(8,128)}, u32[]{:S(2)}) copy-start(f32[32,32]{1,0:T(8,128)} %reshape.254) | copy-start | bytes 12292
  740.1 247.3 %copy-start.48 = (f32[32,32]{1,0:T(8,128)S(1)}, f32[32,32]{1,0:T(8,128)}, u32[]{:S(2)}) copy-start(f32[32,32]{1,0:T(8,128)} %reshape.253) | copy-start | bytes 12292
  740.1 247.5 %copy-start.46 = (f32[32,32]{1,0:T(8,128)S(1)}, f32[32,32]{1,0:T(8,128)}, u32[]{:S(2)}) copy-start(f32[32,32]{1,0:T(8,128)} %reshape.252) | copy-start | bytes 12292
  740.1 247.6 %copy-start.44 = (f32[32,32]{1,0:T(8,128)S(1)}, f32[32,32]{1,0:T(8,128)}, u32[]{:S(2)}) copy-start(f32[32,32]{1,0:T(8,128)} %copy-done.42) | copy-start | bytes 12292
  740.2 247.8 %copy-start.32 = (f32[2,32,32]{2,1,0:T(8,128)S(1)}, f32[2,32,32]{2,1,0:T(8,128)}, u32[]{:S(2)}) copy-start(f32[2,32,32]{2,1,0:T(8,128)} %copy-done.30) | copy-start | bytes 24580
  740.2 247.9 %copy-start.22 = (f32[4,32,32]{2,1,0:T(8,128)S(1)}, f32[4,32,32]{2,1,0:T(8,128)}, u32[]{:S(2)}) copy-start(f32[4,32,32]{2,1,0:T(8,128)} %copy-done.20) | copy-start | bytes 49156
  740.2 248.4 %copy-start.11 = (f32[8,64,32]{2,1,0:T(8,128)S(1)}, f32[8,64,32]{2,1,0:T(8,128)}, u32[]{:S(2)}) copy-start(f32[8,64,32]{2,1,0:T(8,128)} %copy-done.9) | copy-start | bytes 196612
  (37 other events, 118.0 us)
Sparse Core Ops, SparseCore 0:
  14.8 106.7 all-gather.4
  230.2 260.5 all-reduce.2
  506.1 102.4 all-gather.6
  718.1 260.5 all-reduce.4
where the time goes:
time: 1000 us; the launch traced here: 997 us
  waiting for transfers between devices  588 us (59%)
  local copies, waits for them, and re-layouts  284 us (28%)
  matrix products  52.9 us (5%)
  other arithmetic  36.2 us (4%)
  starting transfers between devices  20.4 us (2%)
  between operations  15.5 us (2%)
    psum x2, waiting for transfers between devices, apply_operator(): lax.psum(upper_far.reshape(-1, RANK * NRHS), 'dev').reshape(-1, RANK, NRHS)  473 us
    slice x4, local copies, waits for them, and re-layouts, apply_operator(): upper_levels = [gathered[0::2] + gathered[1::2]]  146 us
    all_gather x2, waiting for transfers between devices, apply_operator(): lax.all_gather(parent_share.reshape(1, RANK * NRHS), 'dev', axis=0, tiled...  115 us
    dot_general x52, matrix products, product(): return jnp.einsum(form, left, right, precision=highest)  52.9 us
    unnamed x174, local copies, waits for them, and re-layouts  24 us
  transfers between devices with their start and end apart: 12, of which 4 were waited for; matrix products, arithmetic and copies ran while one was open for 34% of the time, Pallas kernels for 0%

commit v1 on v0

v1 whole, which is shorter than its diff:
```python
import jax
import jax.numpy as jnp
import numpy as np
from jax import lax
from jax.experimental import pallas as pl
from jax.experimental.pallas import tpu as pltpu
from jax.sharding import PartitionSpec as P

NRHS = 64
LEAF = 64
RANK = 32
NEARP = 12
FARP = 8
L_DEV = 8
CPD = 15
NW = 2
DEVICES = 256
CHIPS = 128
LEVELS = (128, 64, 32, 16, 8, 4, 2)
UPC = 254
UPE = 252
HOLD = 4
RECORDS = CHIPS * HOLD
ROWS = L_DEV * LEAF
COEF = CPD * RANK
HALF = NRHS // 2
RIM = NW * LEAF
MEMORY = pltpu.CompilerParams(vmem_limit_bytes=56 * 1024 * 1024)

def split(array):
    high = array.astype(jnp.bfloat16)
    return high, (array - high.astype(jnp.float32)).astype(jnp.bfloat16)


def dot(left, right):
    return jnp.dot(left, right, preferred_element_type=jnp.float32)


def mul(left, right):
    lh, ll = split(left)
    rh, rl = split(right)
    return dot(lh, rh) + (dot(lh, rl) + dot(ll, rh))


def first_of(m):
    return DEVICES - 2 * m


def ring(stride, size, step):
    pairs = []
    for i in range(DEVICES):
        at = (i // stride) % size
        pairs.append((i, i + ((at + step) % size - at) * stride))
    return pairs


STAGES = ((8, 2), (16, 4), (64, 4), (2, 4))


def join_kernel(*refs):
    out_ref = refs[-1]
    at = 0
    for ref in refs[:-1]:
        out_ref[at : at + ref.shape[0]] = ref[...]
        at += ref.shape[0]


def join(parts):
    shape = (sum(p.shape[0] for p in parts),) + parts[0].shape[1:]
    return call(join_kernel, [f32(*shape)], parts)[0]


def gather_chips(piece):
    parts = [piece]
    for stride, size in STAGES:
        if len(parts) > 1:
            piece = join(parts)
        parts = [piece] + [
            lax.ppermute(piece, "dev", ring(stride, size, step)) for step in range(1, size)
        ]
    return parts


def gathered_chip(me, place):
    chip = me // 2
    x = (chip - place // 32) & 3
    low = (chip // 4 - place % 2) & 1
    high = (chip // 8 - place // 2 % 4) & 3
    y = (chip // 32 - place // 8 % 4) & 3
    return y * 32 + high * 8 + low * 4 + x


def other_core(array):
    return lax.ppermute(array, "dev", ring(1, 2, 1))


def neighbours(array_up, array_down):
    up = [(i, i + 1) for i in range(DEVICES - 1)]
    down = [(i + 1, i) for i in range(DEVICES - 1)]
    return lax.ppermute(array_up, "dev", up), lax.ppermute(array_down, "dev", down)


def call(kernel, outs, ins, scratch=(), smem=0, flops=1_000_000, size=1_000_000):
    vmem = pl.BlockSpec(memory_space=pltpu.VMEM)
    scalar = pl.BlockSpec(memory_space=pltpu.SMEM)
    return pl.pallas_call(
        kernel,
        out_shape=[jax.ShapeDtypeStruct(s, d) for s, d in outs],
        in_specs=[scalar] * smem + [vmem] * (len(ins) - smem),
        out_specs=[vmem] * len(outs),
        scratch_shapes=list(scratch),
        compiler_params=MEMORY,
        cost_estimate=pl.CostEstimate(flops=flops, bytes_accessed=size, transcendentals=0),
    )(*ins)


def f32(*shape):
    return (shape, jnp.float32)


def pack(matrix):
    return jnp.concatenate([matrix[8 * g : 8 * g + 8] for g in range(4)], axis=1)


def unpack(tile):
    return jnp.concatenate([tile[:, g * RANK : (g + 1) * RANK] for g in range(4)], axis=0)


def pick_half(array, core):
    return jnp.where(core == 0, array[:, :HALF], array[:, HALF:NRHS])


def both_halves(own, other, core):
    return jnp.concatenate(
        [jnp.where(core == 0, own, other), jnp.where(core == 0, other, own)], axis=1
    )


def basis_kernel(v_ref, e_ref, x_ref, low_ref, lowt_ref, top_ref, topt_ref, c_ref, sent_ref):
    bases = [v_ref[...]]
    offset = 0
    breadth = L_DEV
    while breadth >= 1:
        rows = ROWS // breadth
        parts = []
        for p in range(breadth):
            link = e_ref[(offset + p) * RANK : (offset + p + 1) * RANK, :]
            parts.append(mul(bases[-1][p * rows : (p + 1) * rows], link))
        bases.append(jnp.concatenate(parts, axis=0))
        offset += breadth
        breadth //= 2
    blocks = []
    breadth = L_DEV
    for level in bases[:-1]:
        wide = jnp.concatenate([level] * breadth, axis=1)
        row = lax.broadcasted_iota(jnp.int32, wide.shape, 0) // (ROWS // breadth)
        column = lax.broadcasted_iota(jnp.int32, wide.shape, 1) // RANK
        blocks.append(jnp.where(row == column, wide, 0.0))
        breadth //= 2
    whole = jnp.concatenate(blocks + [bases[-1]], axis=1)
    turned = whole.T
    low_ref[...] = whole[:, :COEF]
    top_ref[...] = bases[-1]
    lowt_ref[...] = turned[:COEF]
    topt_ref[...] = turned[COEF:]
    x = x_ref[...]
    everything = mul(turned, jnp.concatenate([x, bases[-1], jnp.zeros((ROWS, 32), jnp.float32)], axis=1))
    c_ref[...] = everything[:COEF, :NRHS]
    sent_ref[...] = everything[COEF:]


def record_kernel(me_ref, own_ref, other_ref, pair_ref, tile_ref, out_ref):
    both = own_ref[...] + other_ref[...]
    out_ref[0, 0:8, :] = pack(pick_half(both, me_ref[0] % 2))
    out_ref[0, 8:16, :] = pair_ref[...]
    out_ref[0, 16:48, :] = tile_ref[...]


def near_kernel(me_ref, count_ref, partner_ref, block_ref, band_ref, total):
    total[...] = jnp.zeros_like(total)
    first = me_ref[0] * L_DEV
    for t in range(L_DEV):
        for s in range(NEARP):

            @pl.when(s < count_ref[t])
            def _(t=t, s=s):
                at = jnp.clip(partner_ref[t, s] - (first + t) + NW, 0, 2 * NW)
                rows = (t * NEARP + s) * LEAF
                total[t, at] += block_ref[rows : rows + LEAF, :]

    for t in range(L_DEV):
        band_ref[t * LEAF : (t + 1) * LEAF, :] = jnp.concatenate(
            [total[t, k] for k in range(2 * NW + 1)], axis=1
        )


def couple_kernel(count_ref, block_ref, out_ref):
    for r in range(CPD):
        parts = []
        for s in range(FARP):
            at = (r * FARP + s) * RANK
            parts.append(jnp.where(s < count_ref[r], block_ref[at : at + RANK, :], 0.0))
        out_ref[r * RANK : (r + 1) * RANK, :] = jnp.concatenate(parts, axis=1)


def local_kernel(
    me_ref, far_ref, band_ref, couple_ref, low_ref, topt_ref, x_ref, c_ref, before_ref, after_ref,
    y_ref, share_ref, xe, ce, far_pick, far_sum
):
    xe[0:RIM, :] = before_ref[COEF:, :]
    xe[RIM : RIM + ROWS, :] = x_ref[...]
    xe[RIM + ROWS :, :] = after_ref[COEF:, :]
    ce[0:COEF, :] = before_ref[:COEF, :]
    ce[COEF : 2 * COEF, :] = c_ref[...]
    ce[2 * COEF :, :] = after_ref[:COEF, :]
    me = me_ref[0]
    r = 0
    breadth = L_DEV
    while breadth >= 1:
        offset = 2 * L_DEV - 2 * breadth
        for _ in range(breadth):
            for s in range(FARP):
                along = jnp.clip(far_ref[r, s] - (me - 1) * breadth, 0, 3 * breadth - 1)
                place = along // breadth * CPD + offset + along % breadth
                at = pl.multiple_of(place * RANK, RANK)
                far_pick[r, s * RANK : (s + 1) * RANK, :] = ce[pl.ds(at, RANK), :]
            r += 1
        breadth //= 2
    for r in range(CPD):
        rows = slice(r * RANK, (r + 1) * RANK)
        far_sum[rows, :] = mul(couple_ref[rows, :], far_pick[r])
    spread = mul(low_ref[...], far_sum[...])
    for t in range(L_DEV):
        rows = slice(t * LEAF, (t + 1) * LEAF)
        window = xe[t * LEAF : (t + 2 * NW + 1) * LEAF, :]
        y_ref[rows, :] = spread[rows] + mul(band_ref[rows, :], window)
    share_ref[...] = mul(topt_ref[...], y_ref[...])


def links_kernel(me_ref, u_ref, q_ref, u3_ref):
    high, low = split(u_ref[...])
    u3_ref[...] = jnp.concatenate([high, low, high], axis=1)
    row = lax.broadcasted_iota(jnp.int32, (128, 128), 0)
    column = lax.broadcasted_iota(jnp.int32, (128, 128), 1)
    same = row // RANK == column // RANK
    product = None
    for k, m in enumerate(LEVELS[:-1]):
        ancestor = first_of(m) + me_ref[0] // (DEVICES // m)
        link = u_ref[pl.ds(pl.multiple_of(ancestor * RANK, RANK), RANK), :]
        product = link if product is None else mul(product, link)
        wide = jnp.concatenate([product.T] * 4, axis=1)
        tall = jnp.concatenate([wide] * 4, axis=0)
        q_ref[k] = jnp.where(same, tall, 0.0)


def fold_kernel(me_ref, p0, p1, p2, p3, q_ref, u3_ref, _, w_ref, t_ref, total, ready, turned):
    pieces = (p0, p1, p2, p3)
    me = me_ref[0]
    per = CHIPS // 4
    for k, piece in enumerate(pieces):
        t_ref[k * per * 8 : (k + 1) * per * 8, :] = piece[:, 0:8, :].reshape(per * 8, 128)
    pairs = jnp.concatenate([piece[:, 8, :] for piece in pieces], axis=0).T
    mask = []
    for j in range(HOLD):
        target = pairs[j : j + 1, :].astype(jnp.int32)
        source = pairs[HOLD + j : HOLD + j + 1, :].astype(jnp.int32)
        wanted = target < 0
        for m in LEVELS:
            wanted = wanted | (target == first_of(m) + me // (DEVICES // m))
        source = jnp.where(wanted, source, -1)
        row = lax.broadcasted_iota(jnp.int32, (256, CHIPS), 0)
        mask.append(jnp.where(row == source, 1.0, 0.0).astype(jnp.bfloat16))
    mask = jnp.concatenate(mask, axis=1)
    for r in range(8):
        rows = jnp.concatenate(
            [piece[:, 16 + 8 * j + r, :] for j in range(HOLD) for piece in pieces], axis=0
        )
        high, low = split(rows)
        both = dot(mask, jnp.concatenate([high, low], axis=1))
        total[:, r, :] = both[:, :128] + both[:, 128:]
    direct = {}
    for k, m in enumerate(LEVELS[1:]):
        o = first_of(m)
        packed = mul(total[o : o + m].reshape(m * 8, 128), q_ref[k])
        for u in range(m):
            direct[m, u] = packed[8 * u : 8 * u + 8]
    above = [unpack(direct[2, u]) for u in range(2)]
    for m in (4, 8, 16, 32, 64, 128):
        o = first_of(m)
        level = []
        for q in range(m // 2):
            high, low = split(above[q])
            stack = jnp.concatenate([high, high, low], axis=0)
            at = (o + 2 * q) * RANK
            grown = dot(u3_ref[at : at + 2 * RANK, :], stack)
            for i in range(2):
                part = grown[i * RANK : (i + 1) * RANK]
                if m < 128:
                    level.append(unpack(direct[m, 2 * q + i]) + part)
                else:
                    ready[2 * q + i] = total[2 * q + i] + pack(part)
        above = level
    for i in range(CHIPS):
        turned[8 * i : 8 * i + 8, :] = ready[gathered_chip(me, i)]
    w_ref[...] = turned[...].T


def diagonal(z):
    return sum(z[g * RANK : (g + 1) * RANK, g * HALF : (g + 1) * HALF] for g in range(4))


def middle_kernel(
    me_ref, w0_ref, w1_ref, t_ref, sent0_ref, sent1_ref, s0_ref, s1_ref, w_ref, ud_ref, next_ref
):
    w = w0_ref[...] + w1_ref[...]
    w_ref[...] = w
    ud = diagonal(mul(w, t_ref[...]))
    ud_ref[...] = ud
    gram = (sent0_ref[...] + sent1_ref[...])[:, NRHS : NRHS + RANK]
    share = pick_half(s0_ref[...] + s1_ref[...], me_ref[0] % 2)
    next_ref[...] = pack(share + mul(gram, ud))


def last_kernel(w_ref, p0, p1, p2, p3, _, ud_ref):
    t = jnp.concatenate([p0[...], p1[...], p2[...], p3[...]], axis=0)
    ud_ref[...] = diagonal(mul(w_ref[...], t))


def finish_up_kernel(me_ref, y_ref, own_ref, other_ref, top_ref, lowt_ref, out_ref, c_ref):
    ud = both_halves(own_ref[...], other_ref[...], me_ref[0] % 2)
    out = y_ref[...] + mul(top_ref[...], ud)
    out_ref[...] = out
    c_ref[...] = mul(lowt_ref[...], out)


def finish_kernel(me_ref, y_ref, own_ref, other_ref, top_ref, out_ref):
    ud = both_halves(own_ref[...], other_ref[...], me_ref[0] % 2)
    out_ref[...] = y_ref[...] + mul(top_ref[...], ud)


def body(
    block_in, leaf_basis, transfer, upper_transfer, near_count, near_partner, near_block,
    far_count, far_partner, coupling, upper_pair, upper_block
):
    me = lax.axis_index("dev").reshape(1)

    vectors = block_in.reshape(ROWS, NRHS)
    low, lowt, top, topt, coefs, sent = call(
        basis_kernel,
        [f32(ROWS, COEF), f32(COEF, ROWS), f32(ROWS, RANK), f32(RANK, ROWS), f32(COEF, NRHS), f32(RANK, 128)],
        [leaf_basis.reshape(ROWS, RANK), transfer.reshape(COEF, RANK), vectors],
        flops=100_000_000,
    )
    sent_other = other_core(sent)

    tiles = upper_block.reshape(HOLD, RANK, 4, 8).transpose(0, 3, 2, 1).reshape(HOLD * 8, 128)
    pairs = jnp.pad(
        upper_pair.astype(jnp.float32).T.reshape(1, 2 * HOLD), ((0, 7), (0, 128 - 2 * HOLD))
    )
    (record,) = call(record_kernel, [f32(1, 48, 128)], [me, sent, sent_other, pairs, tiles], smem=1)
    pieces = gather_chips(record)

    q, links = call(
        links_kernel,
        [f32(6, 128, 128), ((UPE * RANK, 96), jnp.bfloat16)],
        [me, upper_transfer.reshape(UPE * RANK, RANK)],
        smem=1,
    )
    (band,) = call(
        near_kernel,
        [f32(ROWS, (2 * NW + 1) * LEAF)],
        [me, near_count, near_partner, near_block.reshape(L_DEV * NEARP * LEAF, LEAF)],
        scratch=[pltpu.VMEM((L_DEV, 2 * NW + 1, LEAF, LEAF), jnp.float32)],
        smem=3,
    )
    (couple,) = call(
        couple_kernel,
        [f32(COEF, FARP * RANK)],
        [far_count, coupling.reshape(CPD * FARP * RANK, RANK)],
        smem=1,
    )

    def local(x, c):
        before, after = neighbours(
            jnp.concatenate([c, x[ROWS - RIM :]], axis=0), jnp.concatenate([c, x[:RIM]], axis=0)
        )
        return call(
            local_kernel,
            [f32(ROWS, NRHS), f32(RANK, NRHS)],
            [me, far_partner, band, couple, low, topt, x, c, before, after],
            scratch=[
                pltpu.VMEM((ROWS + 2 * RIM, NRHS), jnp.float32),
                pltpu.VMEM((3 * COEF, NRHS), jnp.float32),
                pltpu.VMEM((CPD, FARP * RANK, NRHS), jnp.float32),
                pltpu.VMEM((COEF, NRHS), jnp.float32),
            ],
            smem=2,
            flops=300_000_000,
            size=4_000_000,
        )

    near_first, share = local(vectors, coefs)
    share_other = other_core(share)

    w_own, first_coefs = call(
        fold_kernel,
        [f32(128, CHIPS * 8), f32(CHIPS * 8, 128)],
        [me, *pieces, q, links, share],
        scratch=[
            pltpu.VMEM((256, 8, 128), jnp.float32),
            pltpu.VMEM((CHIPS, 8, 128), jnp.float32),
            pltpu.VMEM((CHIPS * 8, 128), jnp.float32),
        ],
        smem=1,
        flops=100_000_000,
    )
    w, ud, second_record = call(
        middle_kernel,
        [f32(128, CHIPS * 8), f32(RANK, HALF), f32(8, 128)],
        [me, w_own, other_core(w_own), first_coefs, sent, sent_other, share, share_other],
        smem=1,
        flops=100_000_000,
    )
    second_pieces = gather_chips(second_record)

    first_rows, coefs_second = call(
        finish_up_kernel,
        [f32(ROWS, NRHS), f32(COEF, NRHS)],
        [me, near_first, ud, other_core(ud), top, lowt],
        smem=1,
        flops=100_000_000,
    )
    near_second, after = local(first_rows, coefs_second)
    (ud,) = call(last_kernel, [f32(RANK, HALF)], [w, *second_pieces, after], flops=100_000_000)
    (second_rows,) = call(
        finish_kernel, [f32(ROWS, NRHS)], [me, near_second, ud, other_core(ud), top], smem=1
    )
    return (
        first_rows.reshape(L_DEV, LEAF * NRHS),
        second_rows.reshape(L_DEV, LEAF * NRHS),
    )


def solution(mesh):
    in_specs = (
        P("dev", None),
        P("dev", None),
        P("dev", None),
        P(),
        P("dev"),
        P("dev", None),
        P("dev", None, None),
        P("dev"),
        P("dev", None),
        P("dev", None, None),
        P("dev", None),
        P("dev", None),
    )
    out_specs = (P("dev", None), P("dev", None))
    return jax.shard_map(body, mesh=mesh, in_specs=in_specs, out_specs=out_specs, check_vma=False)
```

time: 1000 us -> 175 us (0.17)
  waiting for transfers between devices: 588 us -> 28.9 us
  local copies, waits for them, and re-layouts: 284 us -> 32.3 us
  Pallas kernels: 0 us -> 53.9 us
  matrix products: 52.9 us -> 0 us
  starting transfers between devices: 20.4 us -> 54 us
  other arithmetic: 36.2 us -> 2.63 us
  between operations: 15.5 us -> 0.85 us
    psum x2 -> x0, waiting for transfers between devices: 473 us -> none  [apply_operator(): lax.psum(upper_far.reshape(-1, RANK * NRHS), 'dev').reshape(-1, RANK, NRHS)]
    slice x28 -> x4, local copies, waits for them, and re-layouts: 157 us -> 1.12 us  [the longest x3 1.01 us: local(): x[:RIM]]
    all_gather x2 -> x0, waiting for transfers between devices: 115 us -> none  [apply_operator(): lax.all_gather(parent_share.reshape(1, RANK * NRHS), 'dev', axis=0, tiled...]
    pallas_call x0 -> x18, Pallas kernels: none -> 53.9 us  [call(): pl.pallas_call(kernel, out_shape=[jax.ShapeDtypeStruct(s, d) for s, d in...]
    dot_general x52 -> x0, matrix products: 52.9 us -> none  [product(): return jnp.einsum(form, left, right, precision=highest)]
    ppermute x8 -> x29, starting transfers between devices: 20.1 us -> 54 us  [the longest x20 40.3 us: gather_chips(): lax.ppermute(piece, 'dev', ring(stride, size, step))]
    ppermute x8 -> x29, waiting for transfers between devices: 0.02 us -> 28.9 us  [the longest x20 22.7 us: gather_chips(): lax.ppermute(piece, 'dev', ring(stride, size, step))]
    reshape x31 -> x11, local copies, waits for them, and re-layouts: 42.9 us -> 17 us  [the longest x1 3.32 us: body(): upper_transfer.reshape(UPE * RANK, RANK)]
  transfers between devices with their start and end apart: 12 -> 29, of which waited for: 4 -> 17; matrix products, arithmetic and copies ran while one was open for 34% -> 9% of each run, Pallas kernels for 0% -> 15%
where the time goes in v1:
time: 175 us; the launch traced here: 173 us
  starting transfers between devices  54 us (31%)
  Pallas kernels  53.9 us (31%)
  local copies, waits for them, and re-layouts  32.3 us (18%)
  waiting for transfers between devices  28.9 us (17%)
  other arithmetic  2.63 us (2%)
    pallas_call x18, Pallas kernels, call(): pl.pallas_call(kernel, out_shape=[jax.ShapeDtypeStruct(s, d) for s, d in...  53.9 us
    ppermute x20, starting transfers between devices, gather_chips(): lax.ppermute(piece, 'dev', ring(stride, size, step))  40.3 us
    ppermute x20, waiting for transfers between devices, gather_chips(): lax.ppermute(piece, 'dev', ring(stride, size, step))  22.7 us
    unnamed x68, local copies, waits for them, and re-layouts  13.4 us
    ppermute x2, starting transfers between devices, neighbours(): lax.ppermute(array_down, 'dev', down)  7.14 us
    ppermute x2, starting transfers between devices, neighbours(): lax.ppermute(array_up, 'dev', up)  4.15 us
  transfers between devices with their start and end apart: 29, of which 17 were waited for; matrix products, arithmetic and copies ran while one was open for 9% of the time, Pallas kernels for 15%

profile of v1, /device:TPU:2, one launch (start us, length us, event | category | flops | bytes accessed | tf_op | source)
XLA Modules:
  0.0 172.6 jit_solution(1376084091995999377)
XLA Ops:
  0.6 1.7 reshape.47.x_ref
  2.3 1.7 reshape.45.v_ref
  4.0 1.7 reshape.46.e_ref
  5.7 3.7 %shard_map.133 = (f32[512,480]{1,0:T(8,128)}, f32[480,512]{1,0:T(8,128)}, f32[512,32]{1,0:T(8,128)}, f32[32,512]{1,0:T(8,128)}, f32[480,64]{1,0:T(8,128)}, /*index=5*/f32[32,128]{1,0:T(8,128)}) custom-call(f32[512,32]{1,0:T(8,128)} %reshape.45.v_ref, f32[480,32]{1,0:T(8,128)} %reshape.46.e_ref, f32[512,64]{1,0:T(8,128)} %reshape.47.x_ref), custom_call_target="tpu_custom_call" | custom-call | flops 100000000 | bytes 1000000 | tf_op jit(solution)/shard_map/pallas_call | solution.py:106
  10.1 1.1 reshape.49
  13.3 1.5 shard_map.135.refs_0_
  14.8 1.9 %collective-permute-start.3 = (f32[1,48,128]{2,1,0:T(8,128)}, f32[1,48,128]{2,1,0:T(8,128)S(1)}, u32[]{:S(2)}, u32[]{:S(2)}) collective-permute-start(f32[1,48,128]{2,1,0:T(8,128)} %shard_map.135.refs_0_), channel_id=1, source_target_pairs={{0,8},{1,9},{2,10},{3,11},{4,12},{5,13},{6,14},{7,15},{8,0},{9,1},... | collective-permute-start | bytes 73736 | tf_op jit(solution)/shard_map/ppermute | solution.py:79
  16.7 2.1 %collective-permute-done.3.refs_1_ = f32[1,48,128]{2,1,0:T(8,128)S(1)} collective-permute-done((f32[1,48,128]{2,1,0:T(8,128)}, f32[1,48,128]{2,1,0:T(8,128)S(1)}, u32[]{:S(2)}, u32[]{:S(2)}) %collective-permute-start.3) | collective-permute-done | bytes 24608 | tf_op jit(solution)/shard_map/ppermute | solution.py:79
  19.5 1.4 shard_map.136.refs_0_
  20.9 3.3 %collective-permute-start.4 = (f32[2,48,128]{2,1,0:T(8,128)}, f32[2,48,128]{2,1,0:T(8,128)S(1)}, u32[]{:S(2)}, u32[]{:S(2)}) collective-permute-start(f32[2,48,128]{2,1,0:T(8,128)} %shard_map.136.refs_0_), channel_id=1, source_target_pairs={{0,16},{1,17},{2,18},{3,19},{4,20},{5,21},{6,22},{7,23},{8,24},{9,... | collective-permute-start | bytes 147464 | tf_op jit(solution)/shard_map/ppermute | solution.py:79
  24.1 5.4 %collective-permute-start.5 = (f32[2,48,128]{2,1,0:T(8,128)}, f32[2,48,128]{2,1,0:T(8,128)S(1)}, u32[]{:S(2)}, u32[]{:S(2)}) collective-permute-start(f32[2,48,128]{2,1,0:T(8,128)} %shard_map.136.refs_0_), channel_id=1, source_target_pairs={{0,32},{1,33},{2,34},{3,35},{4,36},{5,37},{6,38},{7,39},{8,40},{9,... | collective-permute-start | bytes 147464 | tf_op jit(solution)/shard_map/ppermute | solution.py:79
  29.5 2.7 %collective-permute-start.6 = (f32[2,48,128]{2,1,0:T(8,128)}, f32[2,48,128]{2,1,0:T(8,128)S(1)}, u32[]{:S(2)}, u32[]{:S(2)}) collective-permute-start(f32[2,48,128]{2,1,0:T(8,128)} %shard_map.136.refs_0_), channel_id=1, source_target_pairs={{0,48},{1,49},{2,50},{3,51},{4,52},{5,53},{6,54},{7,55},{8,56},{9,... | collective-permute-start | bytes 147464 | tf_op jit(solution)/shard_map/ppermute | solution.py:79
  32.9 1.8 %collective-permute-done.6.refs_3_ = f32[2,48,128]{2,1,0:T(8,128)S(1)} collective-permute-done((f32[2,48,128]{2,1,0:T(8,128)}, f32[2,48,128]{2,1,0:T(8,128)S(1)}, u32[]{:S(2)}, u32[]{:S(2)}) %collective-permute-start.6) | collective-permute-done | bytes 49184 | tf_op jit(solution)/shard_map/ppermute | solution.py:79
  35.3 1.6 shard_map.137.refs_0_
  36.9 1.6 collective-permute-start.7
  38.5 2.9 %collective-permute-start.8 = (f32[8,48,128]{2,1,0:T(8,128)}, f32[8,48,128]{2,1,0:T(8,128)S(1)}, u32[]{:S(2)}, u32[]{:S(2)}) collective-permute-start(f32[8,48,128]{2,1,0:T(8,128)} %shard_map.137.refs_0_), channel_id=1, source_target_pairs={{0,128},{1,129},{2,130},{3,131},{4,132},{5,133},{6,134},{7,135},{8... | collective-permute-start | bytes 589832 | tf_op jit(solution)/shard_map/ppermute | solution.py:79
  41.4 1.3 collective-permute-start.9
  42.7 2.6 %collective-permute-done.7.refs_1_ = f32[8,48,128]{2,1,0:T(8,128)S(1)} collective-permute-done((f32[8,48,128]{2,1,0:T(8,128)}, f32[8,48,128]{2,1,0:T(8,128)S(1)}, u32[]{:S(2)}, u32[]{:S(2)}) %collective-permute-start.7) | collective-permute-done | bytes 196640 | tf_op jit(solution)/shard_map/ppermute | solution.py:79
  45.3 4.0 %collective-permute-done.8.refs_2_ = f32[8,48,128]{2,1,0:T(8,128)S(1)} collective-permute-done((f32[8,48,128]{2,1,0:T(8,128)}, f32[8,48,128]{2,1,0:T(8,128)S(1)}, u32[]{:S(2)}, u32[]{:S(2)}) %collective-permute-start.8) | collective-permute-done | bytes 196640 | tf_op jit(solution)/shard_map/ppermute | solution.py:79
  50.6 2.2 %shard_map.138.p0 = f32[32,48,128]{2,1,0:T(8,128)} custom-call(f32[8,48,128]{2,1,0:T(8,128)} %shard_map.137.refs_0_, f32[8,48,128]{2,1,0:T(8,128)} %copy-done.9, f32[8,48,128]{2,1,0:T(8,128)} %copy-done.10, f32[8,48,128]{2,1,0:T(8,128)} %copy-done.11), custom_call_target="tpu_custom_call" | custom-call | flops 1000000 | bytes 1000000 | tf_op jit(solution)/shard_map/pallas_call | solution.py:106
  52.8 1.3 collective-permute-start.10
  54.1 1.3 collective-permute-start.11
  55.4 2.1 %collective-permute-start.12 = (f32[32,48,128]{2,1,0:T(8,128)}, f32[32,48,128]{2,1,0:T(8,128)}, u32[]{:S(2)}, u32[]{:S(2)}) collective-permute-start(f32[32,48,128]{2,1,0:T(8,128)} %shard_map.138.p0), channel_id=1, source_target_pairs={{0,6},{1,7},{2,0},{3,1},{4,2},{5,3},{6,4},{7,5},{8,14},{9,15},{10,... | collective-permute-start | bytes 2359304 | tf_op jit(solution)/shard_map/ppermute | solution.py:79
  57.8 0.9 pad_maximum_fusion
  58.7 1.9 %collective-permute-start = (f32[608,64]{1,0:T(8,128)}, f32[608,64]{1,0:T(8,128)}, u32[]{:S(2)}, u32[]{:S(2)}) collective-permute-start(f32[608,64]{1,0:T(8,128)} %get-tuple-element.45), channel_id=1, source_target_pairs={{0,1},{1,2},{2,3},{3,4},{4,5},{5,6},{6,7},{7,8},{8,9},{9,10},{10,1... | collective-permute-start | bytes 466952 | tf_op jit(solution)/shard_map/ppermute | solution.py:100
  60.6 3.8 %collective-permute-start.1 = (f32[608,64]{1,0:T(8,128)}, f32[608,64]{1,0:T(8,128)}, u32[]{:S(2)}, u32[]{:S(2)}) collective-permute-start(f32[608,64]{1,0:T(8,128)} %get-tuple-element.44), channel_id=1, source_target_pairs={{1,0},{2,1},{3,2},{4,3},{5,4},{6,5},{7,6},{8,7},{9,8},{10,9},{11,1... | collective-permute-start | bytes 466952 | tf_op jit(solution)/shard_map/ppermute | solution.py:100
  64.5 2.3 %copy.18 = f32[8,12,4096]{2,1,0:T(8,128)S(1)} copy(f32[8,12,4096]{2,0,1:T(8,128)} %param.18) | data formatting | bytes 3145728 | tf_op args[6]
  66.8 2.4 %reshape.43.block_ref = f32[6144,64]{1,0:T(8,128)} reshape(f32[8,12,4096]{2,1,0:T(8,128)S(1)} %copy.18) | data formatting | bytes 3145728 | tf_op jit(solution)/shard_map/reshape | solution.py:372
  69.2 1.9 %reshape.44.block_ref = f32[3840,32]{1,0:T(8,128)} reshape(f32[15,8,1024]{2,1,0:T(8,128)S(1)} %copy-done.5) | data formatting | bytes 983040 | tf_op jit(solution)/shard_map/reshape | solution.py:379
  71.8 3.3 %reshape.51.u_ref = f32[8064,32]{1,0:T(8,128)} reshape(f32[252,1024]{1,0:T(8,128)S(1)} %copy-done.1) | data formatting | bytes 2064384 | tf_op jit(solution)/shard_map/reshape | solution.py:366
  75.1 4.9 %shard_map.139 = (f32[6,128,128]{2,1,0:T(8,128)}, bf16[8064,96]{1,0:T(8,128)(2,1)}) custom-call(s32[1]{0:T(128)} %bitcast.me_ref, f32[8064,32]{1,0:T(8,128)} %reshape.51.u_ref), custom_call_target="tpu_custom_call" | custom-call | flops 1000000 | bytes 1000000 | tf_op jit(solution)/shard_map/pallas_call | solution.py:106
  80.0 2.8 %shard_map.132.couple_ref = f32[480,256]{1,0:T(8,128)} custom-call(s32[15]{0:T(128)} %count_ref.3, f32[3840,32]{1,0:T(8,128)} %reshape.44.block_ref), custom_call_target="tpu_custom_call" | custom-call | flops 1000000 | bytes 1000000 | tf_op jit(solution)/shard_map/pallas_call | solution.py:106
  82.8 4.4 %shard_map.131.band_ref = f32[512,320]{1,0:T(8,128)} custom-call(s32[1]{0:T(128)} %bitcast.me_ref, s32[8]{0:T(128)} %count_ref.2, s32[8,12]{1,0:T(8,128)} %partner_ref.1, f32[6144,64]{1,0:T(8,128)} %reshape.43.block_ref), custom_call_target="tpu_custom_call" | custom-call | flops 1000000 | bytes 1000000 | tf_op jit(solution)/shard_map/pallas_call | solution.py:106
  87.1 2.9 %collective-permute-done.before_ref = f32[608,64]{1,0:T(8,128)} collective-permute-done((f32[608,64]{1,0:T(8,128)}, f32[608,64]{1,0:T(8,128)}, u32[]{:S(2)}, u32[]{:S(2)}) %collective-permute-start) | collective-permute-done | bytes 155680 | tf_op jit(solution)/shard_map/ppermute | solution.py:100
  90.1 4.7 %shard_map.134 = (f32[512,64]{1,0:T(8,128)}, f32[32,64]{1,0:T(8,128)}) custom-call(s32[1]{0:T(128)} %bitcast.me_ref, s32[15,8]{1,0:T(8,128)} %copy.19.far_ref, f32[512,320]{1,0:T(8,128)} %shard_map.131.band_ref, f32[480,256]{1,0:T(8,128)} %shard_map.132.couple_ref, f32[512,480]{1,0:T(8,128)} %get-tuple-element.21.low_ref, ...), custom_call_target="tpu_custom_call" | custom-call | flops 300000000 | bytes 4000000 | tf_op jit(solution)/shard_map/pallas_call | solution.py:106
  94.8 0.8 copy-done.3
  95.7 7.9 %shard_map.140 = (f32[128,1024]{1,0:T(8,128)}, f32[1024,128]{1,0:T(8,128)}) custom-call(s32[1]{0:T(128)} %bitcast.me_ref, f32[32,48,128]{2,1,0:T(8,128)} %shard_map.138.p0, f32[32,48,128]{2,1,0:T(8,128)} %copy-done.3, f32[32,48,128]{2,1,0:T(8,128)} %collective-permute-done.11.p2, f32[32,48,128]{2,1,0:T(8,128)} %collective-permute-done.12.p3, ...), custom_call_target="tpu_custom_call" | custom-call | flops 100000000 | bytes 1000000 | tf_op jit(solution)/shard_map/pallas_call | solution.py:106
  103.6 2.0 %collective-permute-start.13 = (f32[128,1024]{1,0:T(8,128)}, f32[128,1024]{1,0:T(8,128)S(1)}, u32[]{:S(2)}, u32[]{:S(2)}) collective-permute-start(f32[128,1024]{1,0:T(8,128)} %get-tuple-element.29.w0_ref), channel_id=1, source_target_pairs={{0,1},{1,0},{2,3},{3,2},{4,5},{5,4},{6,7},{7,6},{8,9},{9,8},{10,11... | collective-permute-start | bytes 1572872 | tf_op jit(solution)/shard_map/ppermute | solution.py:94
  105.6 1.5 collective-permute-done.14.s1_ref
  108.1 2.7 %shard_map.141 = (f32[128,1024]{1,0:T(8,128)}, f32[32,32]{1,0:T(8,128)}, f32[8,128]{1,0:T(8,128)}) custom-call(s32[1]{0:T(128)} %bitcast.me_ref, f32[128,1024]{1,0:T(8,128)} %get-tuple-element.29.w0_ref, f32[128,1024]{1,0:T(8,128)} %copy-done.4, f32[1024,128]{1,0:T(8,128)} %get-tuple-element.30.t_ref, f32[32,128]{1,0:T(8,128)} %get-tuple-element.25.own_ref.sent0_ref, ...), custom_call_target="tpu_custom_call" | custom-call | flops 100000000 | bytes 1000000 | tf_op jit(solution)/shard_map/pallas_call | solution.py:106
  111.1 1.0 collective-permute-done.15.other_ref
  112.8 3.1 %shard_map.142 = (f32[512,64]{1,0:T(8,128)}, f32[480,64]{1,0:T(8,128)}) custom-call(s32[1]{0:T(128)} %bitcast.me_ref, f32[512,64]{1,0:T(8,128)} %get-tuple-element.24.y_ref, f32[32,32]{1,0:T(8,128)} %get-tuple-element.31.own_ref, f32[32,32]{1,0:T(8,128)} %copy-done.25, f32[512,32]{1,0:T(8,128)} %get-tuple-element.32.top_ref, ...), custom_call_target="tpu_custom_call" | custom-call | flops 100000000 | bytes 1000000 | tf_op jit(solution)/shard_map/pallas_call | solution.py:106
  115.9 0.9 fusion
  116.8 1.0 pad_maximum_fusion.2
  117.8 2.2 %collective-permute-start.16 = (f32[608,64]{1,0:T(8,128)S(1)}, f32[608,64]{1,0:T(8,128)S(1)}, u32[]{:S(2)}, u32[]{:S(2)}) collective-permute-start(f32[608,64]{1,0:T(8,128)S(1)} %get-tuple-element.43), channel_id=1, source_target_pairs={{0,1},{1,2},{2,3},{3,4},{4,5},{5,6},{6,7},{7,8},{8,9},{9,10},{10,1... | collective-permute-start | bytes 466952 | tf_op jit(solution)/shard_map/ppermute | solution.py:100
  120.0 3.3 %collective-permute-start.17 = (f32[608,64]{1,0:T(8,128)S(1)}, f32[608,64]{1,0:T(8,128)S(1)}, u32[]{:S(2)}, u32[]{:S(2)}) collective-permute-start(f32[608,64]{1,0:T(8,128)S(1)} %get-tuple-element.42), channel_id=1, source_target_pairs={{1,0},{2,1},{3,2},{4,3},{5,4},{6,5},{7,6},{8,7},{9,8},{10,9},{11,1... | collective-permute-start | bytes 466952 | tf_op jit(solution)/shard_map/ppermute | solution.py:100
  123.5 3.6 %collective-permute-done.18.refs_1_ = f32[8,128]{1,0:T(8,128)S(1)} collective-permute-done((f32[8,128]{1,0:T(8,128)S(1)}, f32[8,128]{1,0:T(8,128)S(1)}, u32[]{:S(2)}, u32[]{:S(2)}) %collective-permute-start.18) | collective-permute-done | bytes 4128 | tf_op jit(solution)/shard_map/ppermute | solution.py:79
  127.7 1.3 shard_map.144.refs_0_
  128.9 2.2 %collective-permute-start.19 = (f32[16,128]{1,0:T(8,128)}, f32[16,128]{1,0:T(8,128)S(1)}, u32[]{:S(2)}, u32[]{:S(2)}) collective-permute-start(f32[16,128]{1,0:T(8,128)} %shard_map.144.refs_0_), channel_id=1, source_target_pairs={{0,16},{1,17},{2,18},{3,19},{4,20},{5,21},{6,22},{7,23},{8,24},{9,... | collective-permute-start | bytes 24584 | tf_op jit(solution)/shard_map/ppermute | solution.py:79
  131.1 4.1 %collective-permute-start.20 = (f32[16,128]{1,0:T(8,128)}, f32[16,128]{1,0:T(8,128)S(1)}, u32[]{:S(2)}, u32[]{:S(2)}) collective-permute-start(f32[16,128]{1,0:T(8,128)} %shard_map.144.refs_0_), channel_id=1, source_target_pairs={{0,32},{1,33},{2,34},{3,35},{4,36},{5,37},{6,38},{7,39},{8,40},{9,... | collective-permute-start | bytes 24584 | tf_op jit(solution)/shard_map/ppermute | solution.py:79
  135.2 3.7 %collective-permute-done.20.refs_2_ = f32[16,128]{1,0:T(8,128)S(1)} collective-permute-done((f32[16,128]{1,0:T(8,128)}, f32[16,128]{1,0:T(8,128)S(1)}, u32[]{:S(2)}, u32[]{:S(2)}) %collective-permute-start.20) | collective-permute-done | bytes 8224 | tf_op jit(solution)/shard_map/ppermute | solution.py:79
  138.9 1.1 collective-permute-done.21.refs_3_
  140.5 1.3 shard_map.145.refs_0_
  141.9 2.2 %collective-permute-start.22 = (f32[64,128]{1,0:T(8,128)}, f32[64,128]{1,0:T(8,128)S(1)}, u32[]{:S(2)}, u32[]{:S(2)}) collective-permute-start(f32[64,128]{1,0:T(8,128)} %shard_map.145.refs_0_), channel_id=1, source_target_pairs={{0,64},{1,65},{2,66},{3,67},{4,68},{5,69},{6,70},{7,71},{8,72},{9,... | collective-permute-start | bytes 98312 | tf_op jit(solution)/shard_map/ppermute | solution.py:79
  144.1 1.7 collective-permute-start.23
  145.7 1.0 collective-permute-start.24
  147.2 2.5 %collective-permute-done.23.refs_2_ = f32[64,128]{1,0:T(8,128)S(1)} collective-permute-done((f32[64,128]{1,0:T(8,128)}, f32[64,128]{1,0:T(8,128)S(1)}, u32[]{:S(2)}, u32[]{:S(2)}) %collective-permute-start.23) | collective-permute-done | bytes 32800 | tf_op jit(solution)/shard_map/ppermute | solution.py:79
  150.9 1.5 shard_map.146.p0
  152.4 1.3 collective-permute-start.25
  153.6 4.0 %collective-permute-start.26 = (f32[256,128]{1,0:T(8,128)}, f32[256,128]{1,0:T(8,128)S(1)}, u32[]{:S(2)}, u32[]{:S(2)}) collective-permute-start(f32[256,128]{1,0:T(8,128)} %shard_map.146.p0), channel_id=1, source_target_pairs={{0,4},{1,5},{2,6},{3,7},{4,0},{5,1},{6,2},{7,3},{8,12},{9,13},{10,... | collective-permute-start | bytes 393224 | tf_op jit(solution)/shard_map/ppermute | solution.py:79
  159.1 4.7 %shard_map.143 = (f32[512,64]{1,0:T(8,128)}, f32[32,64]{1,0:T(8,128)}) custom-call(s32[1]{0:T(128)} %bitcast.me_ref, s32[15,8]{1,0:T(8,128)} %copy.19.far_ref, f32[512,320]{1,0:T(8,128)} %shard_map.131.band_ref, f32[480,256]{1,0:T(8,128)} %shard_map.132.couple_ref, f32[512,480]{1,0:T(8,128)} %get-tuple-element.21.low_ref, ...), custom_call_target="tpu_custom_call" | custom-call | flops 300000000 | bytes 4000000 | tf_op jit(solution)/shard_map/pallas_call | solution.py:106
  164.5 2.3 %shard_map.147.own_ref = f32[32,32]{1,0:T(8,128)} custom-call(f32[128,1024]{1,0:T(8,128)} %get-tuple-element.37.w_ref, f32[256,128]{1,0:T(8,128)} %shard_map.146.p0, f32[256,128]{1,0:T(8,128)} %copy-done.12, f32[256,128]{1,0:T(8,128)} %copy-done.13, f32[256,128]{1,0:T(8,128)} %copy-done.14, f32[32,64]{1,0:T(8,128)} %get-tuple-element.39._), custom_call_target="tpu_custom_call" | custom-call | flops 100000000 | bytes 1000000 | tf_op jit(solution)/shard_map/pallas_call | solution.py:106
  168.8 2.1 %shard_map.148 = f32[512,64]{1,0:T(8,128)} custom-call(s32[1]{0:T(128)} %bitcast.me_ref, f32[512,64]{1,0:T(8,128)} %get-tuple-element.36.y_ref, f32[32,32]{1,0:T(8,128)} %shard_map.147.own_ref, f32[32,32]{1,0:T(8,128)} %copy-done.26, f32[512,32]{1,0:T(8,128)} %get-tuple-element.32.top_ref), custom_call_target="tpu_custom_call" | custom-call | flops 1000000 | bytes 1000000 | tf_op jit(solution)/shard_map/pallas_call | solution.py:106
  170.9 1.7 reshape.53
  (100 shorter events, 16.4 us)
Async XLA Ops:
  2.3 55.2 %copy-start.8 = (f32[8,4096]{1,0:T(8,128)S(1)}, f32[8,4096]{1,0:T(8,128)}, u32[]{:S(2)}) copy-start(f32[8,4096]{1,0:T(8,128)} %param.12) | copy-start | bytes 393220
  9.4 48.4 %copy-start.2 = (f32[480,64]{1,0:T(8,128)S(1)}, f32[480,64]{1,0:T(8,128)}, u32[]{:S(2)}) copy-start(f32[480,64]{1,0:T(8,128)} %get-tuple-element.23.c_ref) | copy-start | bytes 368644
  9.4 3.3 %collective-permute-start.2 = (f32[32,128]{1,0:T(8,128)}, f32[32,128]{1,0:T(8,128)S(1)}, u32[]{:S(2)}, u32[]{:S(2)}) collective-permute-start(f32[32,128]{1,0:T(8,128)} %get-tuple-element.25.own_ref.sent0_ref), channel_id=1, source_target_pairs={{0,1},{1,0},{2,3},{3,2},{4,5},{5,4},{6,7},{7,6},{8,9},{9,8},{10,11... | collective-permute-start | bytes 49160 | tf_op jit(solution)/shard_map/ppermute | solution.py:94
  12.7 0.6 copy-start.16
  14.8 4.0 %collective-permute-start.3 = (f32[1,48,128]{2,1,0:T(8,128)}, f32[1,48,128]{2,1,0:T(8,128)S(1)}, u32[]{:S(2)}, u32[]{:S(2)}) collective-permute-start(f32[1,48,128]{2,1,0:T(8,128)} %shard_map.135.refs_0_), channel_id=1, source_target_pairs={{0,8},{1,9},{2,10},{3,11},{4,12},{5,13},{6,14},{7,15},{8,0},{9,1},... | collective-permute-start | bytes 73736 | tf_op jit(solution)/shard_map/ppermute | solution.py:79
  18.9 0.6 copy-start.23
  20.9 11.3 %collective-permute-start.4 = (f32[2,48,128]{2,1,0:T(8,128)}, f32[2,48,128]{2,1,0:T(8,128)S(1)}, u32[]{:S(2)}, u32[]{:S(2)}) collective-permute-start(f32[2,48,128]{2,1,0:T(8,128)} %shard_map.136.refs_0_), channel_id=1, source_target_pairs={{0,16},{1,17},{2,18},{3,19},{4,20},{5,21},{6,22},{7,23},{8,24},{9,... | collective-permute-start | bytes 147464 | tf_op jit(solution)/shard_map/ppermute | solution.py:79
  24.1 8.8 %collective-permute-start.5 = (f32[2,48,128]{2,1,0:T(8,128)}, f32[2,48,128]{2,1,0:T(8,128)S(1)}, u32[]{:S(2)}, u32[]{:S(2)}) collective-permute-start(f32[2,48,128]{2,1,0:T(8,128)} %shard_map.136.refs_0_), channel_id=1, source_target_pairs={{0,32},{1,33},{2,34},{3,35},{4,36},{5,37},{6,38},{7,39},{8,40},{9,... | collective-permute-start | bytes 147464 | tf_op jit(solution)/shard_map/ppermute | solution.py:79
  29.5 5.2 %collective-permute-start.6 = (f32[2,48,128]{2,1,0:T(8,128)}, f32[2,48,128]{2,1,0:T(8,128)S(1)}, u32[]{:S(2)}, u32[]{:S(2)}) collective-permute-start(f32[2,48,128]{2,1,0:T(8,128)} %shard_map.136.refs_0_), channel_id=1, source_target_pairs={{0,48},{1,49},{2,50},{3,51},{4,52},{5,53},{6,54},{7,55},{8,56},{9,... | collective-permute-start | bytes 147464 | tf_op jit(solution)/shard_map/ppermute | solution.py:79
  32.2 2.5 %copy-start.17 = (f32[2,48,128]{2,1,0:T(8,128)}, f32[2,48,128]{2,1,0:T(8,128)S(1)}, u32[]{:S(2)}) copy-start(f32[2,48,128]{2,1,0:T(8,128)S(1)} %collective-permute-done.4.refs_1_) | copy-start | bytes 147460
  32.9 1.8 %copy-start.18 = (f32[2,48,128]{2,1,0:T(8,128)}, f32[2,48,128]{2,1,0:T(8,128)S(1)}, u32[]{:S(2)}) copy-start(f32[2,48,128]{2,1,0:T(8,128)S(1)} %collective-permute-done.5.refs_2_) | copy-start | bytes 147460
  34.7 0.6 copy-start.19
  36.9 8.4 %collective-permute-start.7 = (f32[8,48,128]{2,1,0:T(8,128)}, f32[8,48,128]{2,1,0:T(8,128)S(1)}, u32[]{:S(2)}, u32[]{:S(2)}) collective-permute-start(f32[8,48,128]{2,1,0:T(8,128)} %shard_map.137.refs_0_), channel_id=1, source_target_pairs={{0,64},{1,65},{2,66},{3,67},{4,68},{5,69},{6,70},{7,71},{8,72},{9,... | collective-permute-start | bytes 589832 | tf_op jit(solution)/shard_map/ppermute | solution.py:79
  38.5 10.8 %collective-permute-start.8 = (f32[8,48,128]{2,1,0:T(8,128)}, f32[8,48,128]{2,1,0:T(8,128)S(1)}, u32[]{:S(2)}, u32[]{:S(2)}) collective-permute-start(f32[8,48,128]{2,1,0:T(8,128)} %shard_map.137.refs_0_), channel_id=1, source_target_pairs={{0,128},{1,129},{2,130},{3,131},{4,132},{5,133},{6,134},{7,135},{8... | collective-permute-start | bytes 589832 | tf_op jit(solution)/shard_map/ppermute | solution.py:79
  41.4 7.9 %collective-permute-start.9 = (f32[8,48,128]{2,1,0:T(8,128)}, f32[8,48,128]{2,1,0:T(8,128)S(1)}, u32[]{:S(2)}, u32[]{:S(2)}) collective-permute-start(f32[8,48,128]{2,1,0:T(8,128)} %shard_map.137.refs_0_), channel_id=1, source_target_pairs={{0,192},{1,193},{2,194},{3,195},{4,196},{5,197},{6,198},{7,199},{8... | collective-permute-start | bytes 589832 | tf_op jit(solution)/shard_map/ppermute | solution.py:79
  45.3 4.0 %copy-start.9 = (f32[8,48,128]{2,1,0:T(8,128)}, f32[8,48,128]{2,1,0:T(8,128)S(1)}, u32[]{:S(2)}) copy-start(f32[8,48,128]{2,1,0:T(8,128)S(1)} %collective-permute-done.7.refs_1_) | copy-start | bytes 589828
  49.3 0.7 copy-start.10
  49.9 0.7 copy-start.11
  52.8 42.0 %collective-permute-start.10 = (f32[32,48,128]{2,1,0:T(8,128)}, f32[32,48,128]{2,1,0:T(8,128)S(1)}, u32[]{:S(2)}, u32[]{:S(2)}) collective-permute-start(f32[32,48,128]{2,1,0:T(8,128)} %shard_map.138.p0), channel_id=1, source_target_pairs={{0,2},{1,3},{2,4},{3,5},{4,6},{5,7},{6,0},{7,1},{8,10},{9,11},{10,... | collective-permute-start | bytes 2359304 | tf_op jit(solution)/shard_map/ppermute | solution.py:79
  54.1 40.7 %collective-permute-start.11 = (f32[32,48,128]{2,1,0:T(8,128)}, f32[32,48,128]{2,1,0:T(8,128)}, u32[]{:S(2)}, u32[]{:S(2)}) collective-permute-start(f32[32,48,128]{2,1,0:T(8,128)} %shard_map.138.p0), channel_id=1, source_target_pairs={{0,4},{1,5},{2,6},{3,7},{4,0},{5,1},{6,2},{7,3},{8,12},{9,13},{10,... | collective-permute-start | bytes 2359304 | tf_op jit(solution)/shard_map/ppermute | solution.py:79
  55.4 39.4 %collective-permute-start.12 = (f32[32,48,128]{2,1,0:T(8,128)}, f32[32,48,128]{2,1,0:T(8,128)}, u32[]{:S(2)}, u32[]{:S(2)}) collective-permute-start(f32[32,48,128]{2,1,0:T(8,128)} %shard_map.138.p0), channel_id=1, source_target_pairs={{0,6},{1,7},{2,0},{3,1},{4,2},{5,3},{6,4},{7,5},{8,14},{9,15},{10,... | collective-permute-start | bytes 2359304 | tf_op jit(solution)/shard_map/ppermute | solution.py:79
  58.7 31.3 %collective-permute-start = (f32[608,64]{1,0:T(8,128)}, f32[608,64]{1,0:T(8,128)}, u32[]{:S(2)}, u32[]{:S(2)}) collective-permute-start(f32[608,64]{1,0:T(8,128)} %get-tuple-element.45), channel_id=1, source_target_pairs={{0,1},{1,2},{2,3},{3,4},{4,5},{5,6},{6,7},{7,8},{8,9},{9,10},{10,1... | collective-permute-start | bytes 466952 | tf_op jit(solution)/shard_map/ppermute | solution.py:100
  60.6 29.5 %collective-permute-start.1 = (f32[608,64]{1,0:T(8,128)}, f32[608,64]{1,0:T(8,128)}, u32[]{:S(2)}, u32[]{:S(2)}) collective-permute-start(f32[608,64]{1,0:T(8,128)} %get-tuple-element.44), channel_id=1, source_target_pairs={{1,0},{2,1},{3,2},{4,3},{5,4},{6,5},{7,6},{8,7},{9,8},{10,9},{11,1... | collective-permute-start | bytes 466952 | tf_op jit(solution)/shard_map/ppermute | solution.py:100
  66.8 2.4 %copy-start.5 = (f32[15,8,1024]{2,1,0:T(8,128)S(1)}, f32[15,8,1024]{2,1,0:T(8,128)}, u32[]{:S(2)}) copy-start(f32[15,8,1024]{2,1,0:T(8,128)} %param.21) | copy-start | bytes 1474564
  69.2 1.9 %copy-start.30 = (s32[15,8]{0,1:T(8,128)S(1)}, s32[15,8]{0,1:T(8,128)}, u32[]{:S(2)}) copy-start(s32[15,8]{0,1:T(8,128)} %param.20) | copy-start | bytes 1444
  69.2 2.6 %copy-start.1 = (f32[252,1024]{1,0:T(8,128)S(1)}, f32[252,1024]{1,0:T(8,128)}, u32[]{:S(2)}) copy-start(f32[252,1024]{1,0:T(8,128)} %param.15) | copy-start | bytes 3096580
  94.8 0.9 copy-start.3
  95.7 9.9 %copy-start.15 = (f32[32,64]{1,0:T(8,128)S(1)}, f32[32,64]{1,0:T(8,128)}, u32[]{:S(2)}) copy-start(f32[32,64]{1,0:T(8,128)} %get-tuple-element.28._.s0_ref) | copy-start | bytes 24580
  103.6 3.7 %collective-permute-start.13 = (f32[128,1024]{1,0:T(8,128)}, f32[128,1024]{1,0:T(8,128)S(1)}, u32[]{:S(2)}, u32[]{:S(2)}) collective-permute-start(f32[128,1024]{1,0:T(8,128)} %get-tuple-element.29.w0_ref), channel_id=1, source_target_pairs={{0,1},{1,0},{2,3},{3,2},{4,5},{5,4},{6,7},{7,6},{8,9},{9,8},{10,11... | collective-permute-start | bytes 1572872 | tf_op jit(solution)/shard_map/ppermute | solution.py:94
  105.5 1.6 collective-permute-start.14
  107.1 0.6 copy-start.24
  107.3 0.8 copy-start.4
  110.8 12.6 %copy-start.31 = (f32[8,128]{1,0:T(8,128)S(1)}, f32[8,128]{1,0:T(8,128)}, u32[]{:S(2)}) copy-start(f32[8,128]{1,0:T(8,128)} %get-tuple-element.38.refs_0_) | copy-start | bytes 12292
  110.8 1.4 collective-permute-start.15
  112.2 0.6 copy-start.25
  117.8 39.9 %collective-permute-start.16 = (f32[608,64]{1,0:T(8,128)S(1)}, f32[608,64]{1,0:T(8,128)S(1)}, u32[]{:S(2)}, u32[]{:S(2)}) collective-permute-start(f32[608,64]{1,0:T(8,128)S(1)} %get-tuple-element.43), channel_id=1, source_target_pairs={{0,1},{1,2},{2,3},{3,4},{4,5},{5,6},{6,7},{7,8},{8,9},{9,10},{10,1... | collective-permute-start | bytes 466952 | tf_op jit(solution)/shard_map/ppermute | solution.py:100
  120.0 37.6 %collective-permute-start.17 = (f32[608,64]{1,0:T(8,128)S(1)}, f32[608,64]{1,0:T(8,128)S(1)}, u32[]{:S(2)}, u32[]{:S(2)}) collective-permute-start(f32[608,64]{1,0:T(8,128)S(1)} %get-tuple-element.42), channel_id=1, source_target_pairs={{1,0},{2,1},{3,2},{4,3},{5,4},{6,5},{7,6},{8,7},{9,8},{10,9},{11,1... | collective-permute-start | bytes 466952 | tf_op jit(solution)/shard_map/ppermute | solution.py:100
  123.4 3.7 %collective-permute-start.18 = (f32[8,128]{1,0:T(8,128)S(1)}, f32[8,128]{1,0:T(8,128)S(1)}, u32[]{:S(2)}, u32[]{:S(2)}) collective-permute-start(f32[8,128]{1,0:T(8,128)S(1)} %copy-done.31), channel_id=1, source_target_pairs={{0,8},{1,9},{2,10},{3,11},{4,12},{5,13},{6,14},{7,15},{8,0},{9,1},... | collective-permute-start | bytes 12296 | tf_op jit(solution)/shard_map/ppermute | solution.py:79
  127.1 0.6 copy-start.32
  128.9 6.2 %collective-permute-start.19 = (f32[16,128]{1,0:T(8,128)}, f32[16,128]{1,0:T(8,128)S(1)}, u32[]{:S(2)}, u32[]{:S(2)}) collective-permute-start(f32[16,128]{1,0:T(8,128)} %shard_map.144.refs_0_), channel_id=1, source_target_pairs={{0,16},{1,17},{2,18},{3,19},{4,20},{5,21},{6,22},{7,23},{8,24},{9,... | collective-permute-start | bytes 24584 | tf_op jit(solution)/shard_map/ppermute | solution.py:79
  131.1 7.8 %collective-permute-start.20 = (f32[16,128]{1,0:T(8,128)}, f32[16,128]{1,0:T(8,128)S(1)}, u32[]{:S(2)}, u32[]{:S(2)}) collective-permute-start(f32[16,128]{1,0:T(8,128)} %shard_map.144.refs_0_), channel_id=1, source_target_pairs={{0,32},{1,33},{2,34},{3,35},{4,36},{5,37},{6,38},{7,39},{8,40},{9,... | collective-permute-start | bytes 24584 | tf_op jit(solution)/shard_map/ppermute | solution.py:79
  135.2 4.8 %collective-permute-start.21 = (f32[16,128]{1,0:T(8,128)}, f32[16,128]{1,0:T(8,128)S(1)}, u32[]{:S(2)}, u32[]{:S(2)}) collective-permute-start(f32[16,128]{1,0:T(8,128)} %shard_map.144.refs_0_), channel_id=1, source_target_pairs={{0,48},{1,49},{2,50},{3,51},{4,52},{5,53},{6,54},{7,55},{8,56},{9,... | collective-permute-start | bytes 24584 | tf_op jit(solution)/shard_map/ppermute | solution.py:79
  135.2 4.8 %copy-start.27 = (f32[16,128]{1,0:T(8,128)}, f32[16,128]{1,0:T(8,128)S(1)}, u32[]{:S(2)}) copy-start(f32[16,128]{1,0:T(8,128)S(1)} %collective-permute-done.19.refs_1_) | copy-start | bytes 24580
  138.9 1.1 copy-start.28
  139.9 0.6 copy-start.29
  141.9 5.3 %collective-permute-start.22 = (f32[64,128]{1,0:T(8,128)}, f32[64,128]{1,0:T(8,128)S(1)}, u32[]{:S(2)}, u32[]{:S(2)}) collective-permute-start(f32[64,128]{1,0:T(8,128)} %shard_map.145.refs_0_), channel_id=1, source_target_pairs={{0,64},{1,65},{2,66},{3,67},{4,68},{5,69},{6,70},{7,71},{8,72},{9,... | collective-permute-start | bytes 98312 | tf_op jit(solution)/shard_map/ppermute | solution.py:79
  144.1 5.6 %collective-permute-start.23 = (f32[64,128]{1,0:T(8,128)}, f32[64,128]{1,0:T(8,128)S(1)}, u32[]{:S(2)}, u32[]{:S(2)}) collective-permute-start(f32[64,128]{1,0:T(8,128)} %shard_map.145.refs_0_), channel_id=1, source_target_pairs={{0,128},{1,129},{2,130},{3,131},{4,132},{5,133},{6,134},{7,135},{8... | collective-permute-start | bytes 98312 | tf_op jit(solution)/shard_map/ppermute | solution.py:79
  145.7 4.1 %collective-permute-start.24 = (f32[64,128]{1,0:T(8,128)}, f32[64,128]{1,0:T(8,128)S(1)}, u32[]{:S(2)}, u32[]{:S(2)}) collective-permute-start(f32[64,128]{1,0:T(8,128)} %shard_map.145.refs_0_), channel_id=1, source_target_pairs={{0,192},{1,193},{2,194},{3,195},{4,196},{5,197},{6,198},{7,199},{8... | collective-permute-start | bytes 98312 | tf_op jit(solution)/shard_map/ppermute | solution.py:79
  147.2 2.7 %copy-start.20 = (f32[64,128]{1,0:T(8,128)}, f32[64,128]{1,0:T(8,128)S(1)}, u32[]{:S(2)}) copy-start(f32[64,128]{1,0:T(8,128)S(1)} %collective-permute-done.22.refs_1_) | copy-start | bytes 98308
  149.7 0.6 copy-start.21
  150.3 0.6 copy-start.22
  152.4 14.4 %copy-start = (f32[512,64]{1,0:T(8,128)S(1)}, f32[512,64]{1,0:T(8,128)}, u32[]{:S(2)}) copy-start(f32[512,64]{1,0:T(8,128)} %get-tuple-element.34.x_ref) | copy-start | bytes 393220
  152.4 11.4 %collective-permute-start.25 = (f32[256,128]{1,0:T(8,128)}, f32[256,128]{1,0:T(8,128)S(1)}, u32[]{:S(2)}, u32[]{:S(2)}) collective-permute-start(f32[256,128]{1,0:T(8,128)} %shard_map.146.p0), channel_id=1, source_target_pairs={{0,2},{1,3},{2,4},{3,5},{4,6},{5,7},{6,0},{7,1},{8,10},{9,11},{10,... | collective-permute-start | bytes 393224 | tf_op jit(solution)/shard_map/ppermute | solution.py:79
  153.6 10.2 %collective-permute-start.26 = (f32[256,128]{1,0:T(8,128)}, f32[256,128]{1,0:T(8,128)S(1)}, u32[]{:S(2)}, u32[]{:S(2)}) collective-permute-start(f32[256,128]{1,0:T(8,128)} %shard_map.146.p0), channel_id=1, source_target_pairs={{0,4},{1,5},{2,6},{3,7},{4,0},{5,1},{6,2},{7,3},{8,12},{9,13},{10,... | collective-permute-start | bytes 393224 | tf_op jit(solution)/shard_map/ppermute | solution.py:79
  157.6 6.2 %collective-permute-start.27 = (f32[256,128]{1,0:T(8,128)}, f32[256,128]{1,0:T(8,128)S(1)}, u32[]{:S(2)}, u32[]{:S(2)}) collective-permute-start(f32[256,128]{1,0:T(8,128)} %shard_map.146.p0), channel_id=1, source_target_pairs={{0,6},{1,7},{2,0},{3,1},{4,2},{5,3},{6,4},{7,5},{8,14},{9,15},{10,... | collective-permute-start | bytes 393224 | tf_op jit(solution)/shard_map/ppermute | solution.py:79
  157.6 0.7 copy-start.6
  158.4 0.7 copy-start.7
  163.8 0.7 copy-start.12
  163.8 0.7 copy-start.13
  163.8 0.7 copy-start.14
  166.8 1.4 collective-permute-start.28
  168.2 0.6 copy-start.26
